TPU v7x, 128 devices: a whole 4x4x4 slice. The times are simulated.
128 devices in a mesh: tm: 32 (over z, x, y_hi), rows: 4 (over y_lo, core).
Axes of the slice: x: 4, y: 4 (y_hi: 2, y_lo: 2; y = y_hi * 2 + y_lo), z: 4, core: 2. Of those that a mesh axis runs over, the one named last changes fastest.
Arguments:
- video: bfloat16 [256, 32, 128, 128], P('tm', 'rows'), may hold values from -36 to 50
- conv_weight: bfloat16 [3, 3, 3, 128, 256], replicated, may hold values from -0.109375 to 0.109375
- norm_gain: float32 [256], replicated, may hold values from 0.5 to 1.5
- norm_bias: float32 [256], replicated, may hold values from -3 to 3
Outputs:
- patch_tokens: bfloat16 [16, 64, 256, 1024], P('rows', 'tm')
All inputs are finite; a program needn't handle non-finite values.
Results may differ from a plain program's by a relative error of at most 0.0049.
Values may be sent and summed in bfloat16 or wider, within the bound.
A program may use at most 128 MiB of HBM per device.

v0:
```python
import jax
import jax.numpy as jnp
from jax import lax
from jax.sharding import PartitionSpec as P

GROUPS = 32
inv_root = 0.7071067811865476


def from_partner(block, axis, distance):
    count = lax.axis_size(axis)
    route = []
    for low in range(count):
        high = low | 1 << distance
        if high != low and high < count:
            route += [(low, high), (high, low)]
    return lax.ppermute(block, axis, route)


def shifted(block, axis, distance):
    devices = range(lax.axis_size(axis))
    route = [(i - distance, i) for i in devices if i - distance in devices]
    return lax.ppermute(block, axis, route)


def padded_2(cells, sides, width):
    for axis, dim in sides:
        count = lax.axis_size(axis)
        ends = count - 1
        head = lax.slice_in_dim(cells, 0, width, axis=dim)
        tail = lax.slice_in_dim(cells, cells.shape[dim] - width, cells.shape[dim], axis=dim)
        cells = jnp.concatenate(
            [
                lax.ppermute(tail, axis, [(i, (i + 1) % count) for i in range(ends)]),
                cells,
                lax.ppermute(head, axis, [((i + 1) % count, i) for i in range(ends)]),
            ],
            axis=dim,
        )
    return cells


def per_device(video, conv_weight, norm_gain, norm_bias):
    frames, height, width, channels = video.shape
    tm_count = lax.axis_size("tm")
    current = video.astype(jnp.float32)
    position = lax.axis_index("tm")
    for bit_number in range(3):
        partner = from_partner(current, "tm", bit_number)
        is_upper = position >> bit_number & 1 == 1
        current = jnp.where(
            is_upper, (partner - current) * inv_root, (current + partner) * inv_root
        )
    wavelet = current.astype(jnp.bfloat16)
    last_frames = wavelet[frames - 2 :]
    earlier = shifted(last_frames, "tm", 1)
    extended = jnp.concatenate([earlier, wavelet], axis=0)
    with_rows = padded_2(extended, (("rows", 1),), 1)
    padded = jnp.pad(with_rows, ((0, 0), (0, 0), (1, 1), (0, 0)))
    convolved = lax.conv_general_dilated(
        padded[None],
        conv_weight,
        (1, 1, 1),
        "VALID",
        dimension_numbers=("NDHWC", "DHWIO", "NDHWC"),
        preferred_element_type=jnp.float32,
    )[0]
    out_frames, out_height, out_width, out_channels = convolved.shape
    group_count = GROUPS
    groups = convolved.reshape(
        out_frames, out_height, out_width, group_count, out_channels // group_count
    )
    entries = float(
        out_frames
        * out_height
        * out_width
        * (out_channels // group_count)
        * tm_count
        * lax.axis_size("rows")
    )
    local_sums = jnp.sum(groups, axis=(0, 1, 2, 4))
    group_total = lax.psum(local_sums, ("tm", "rows"))
    group_mean = group_total / entries
    centered = groups - group_mean[:, None]
    squares = lax.psum(jnp.sum(centered * centered, axis=(0, 1, 2, 4)), ("tm", "rows"))
    variance = squares / entries
    normed = (centered / jnp.sqrt(variance + 1e-05)[:, None]).reshape(
        out_frames, out_height, out_width, out_channels
    )
    activated = jax.nn.silu(normed * norm_gain + norm_bias).astype(jnp.bfloat16)
    arranged = activated.reshape(
        out_frames, out_height // 2, 2, out_width // 2, 2, out_channels
    ).transpose(1, 3, 0, 2, 4, 5)
    arranged = arranged.reshape(out_height // 2, out_width // 2, out_frames, 4 * out_channels)
    return lax.all_to_all(arranged, "tm", split_axis=1, concat_axis=2, tiled=True)


def solution(mesh):
    placed = (P("tm", "rows", None, None), P(), P(), P())
    return jax.shard_map(
        per_device,
        mesh=mesh,
        in_specs=placed,
        out_specs=P("rows", "tm", None, None),
        check_vma=False,
    )
```

profile of v0, /device:TPU:0, one launch (start us, length us, event | category | flops | bytes accessed | tf_op | source)
XLA Modules:
  0.0 597.1 jit_solution(17662172223809165032)
XLA Ops:
  0.0 4.3 convert_element_type.12
  4.3 3.3 collective-permute-start
  7.5 90.9 %collective-permute-done = f32[8,8,128,128]{3,2,1,0:T(8,128)} collective-permute-done((f32[8,8,128,128]{3,2,1,0:T(8,128)}, f32[8,8,128,128]{3,2,1,0:T(8,128)}, u32[]{:S(2)}, u32[]{:S(2)}) %collective-permute-start) | collective-permute-done | bytes 4194336 | tf_op jit(solution)/shard_map/ppermute | solution.py:17
  98.4 5.9 multiply_select_fusion.1
  104.3 1.5 collective-permute-start.1
  105.9 90.2 %collective-permute-done.1 = f32[8,8,128,128]{3,2,1,0:T(8,128)} collective-permute-done((f32[8,8,128,128]{3,2,1,0:T(8,128)}, f32[8,8,128,128]{3,2,1,0:T(8,128)}, u32[]{:S(2)}, u32[]{:S(2)}) %collective-permute-start.1) | collective-permute-done | bytes 4194336 | tf_op jit(solution)/shard_map/ppermute | solution.py:17
  196.1 6.9 %multiply_select_fusion = f32[8,8,128,128]{3,2,1,0:T(8,128)} fusion(f32[8,8,128,128]{3,2,1,0:T(8,128)} %multiply_select_fusion.1, f32[8,8,128,128]{3,2,1,0:T(8,128)} %collective-permute-done.1, pred[]{:T(512)S(6)} %eq.10), kind=kLoop, calls=%fused_computation.15 | loop fusion | flops 5242880 | bytes 12582913 | tf_op jit(solution)/shard_map/jit(_where)/select_n | solution.py:51
  203.0 3.0 collective-permute-start.2
  206.1 89.3 %collective-permute-done.2 = f32[8,8,128,128]{3,2,1,0:T(8,128)} collective-permute-done((f32[8,8,128,128]{3,2,1,0:T(8,128)}, f32[8,8,128,128]{3,2,1,0:T(8,128)}, u32[]{:S(2)}, u32[]{:S(2)}) %collective-permute-start.2) | collective-permute-done | bytes 4194336 | tf_op jit(solution)/shard_map/ppermute | solution.py:17
  295.4 4.5 select_convert_fusion
  299.9 5.1 collective-permute-start.3
  305.1 8.4 %collective-permute-done.3 = bf16[2,8,128,128]{3,2,1,0:T(8,128)(2,1)S(1)} collective-permute-done((bf16[2,8,128,128]{3,2,1,0:T(8,128)(2,1)S(1)}, bf16[2,8,128,128]{3,2,1,0:T(8,128)(2,1)S(1)}, u32[]{:S(2)}, u32[]{:S(2)}) %collective-permute-start.3) | collective-permute-done | bytes 524320 | tf_op jit(solution)/shard_map/ppermute | solution.py:23
  313.5 1.3 collective-permute-start.4
  314.9 1.3 collective-permute-start.5
  316.2 3.1 collective-permute-done.5
  319.3 2.1 fusion.13
  321.4 2.0 pad.5
  323.4 6.9 %reshape.19 = bf16[10,10,1,8,17,128]{5,4,3,1,0,2:T(8,128)(2,1)} reshape(bf16[10,10,1,136,128]{4,3,1,0,2:T(8,128)(2,1)} %pad.5) | data formatting | bytes 6963200 | tf_op jit(solution)/shard_map/conv_general_dilated | solution.py:60
  330.4 3.0 copy.29
  333.5 19.0 %select_reduce_fusion.1 = (f32[256]{0:T(256)S(1)}, f32[8,8,8,17,256]{4,2,3,1,0:T(8,128)}) fusion(pred[8,17]{0,1:T(8,128)(4,1)S(1)} %copy-done.3, bf16[3,3,3,128,256]{4,3,2,1,0:T(8,128)(2,1)S(1)} %copy-done, bf16[10,10,1,7,2,128]{5,3,4,1,0,2:T(8,128)(2,1)S(1)} %slice.15, bf16[10,10,1,8,17,128]{5,3,4,1,0,2:T(8,128)(2,1)S(1)} %copy.29), kind=kOutput, calls=%fused_computation.3 | convolution fusion | flops 15419842560 | bytes 14523528 | tf_op jit(solution)/shard_map/conv_general_dilated | solution.py:60
  352.8 75.9 %psum.14 = f32[32]{0:T(128)S(1)} all-reduce(f32[32]{0:T(128)S(1)} %reduce_sum.25), channel_id=1, replica_groups=mesh['tm'=32,'rows'=4] {'tm','rows'}, use_global_device_ids=true, to_apply=%region_2.3 | all-reduce | flops 32 | bytes 256 | tf_op jit(solution)/shard_map/psum | solution.py:82
  428.9 6.3 %copy.30 = f32[8,8,8,17,256]{4,1,3,2,0:T(8,128)S(1)} copy(f32[8,8,8,17,256]{4,2,3,1,0:T(8,128)} %get-tuple-element.8) | data formatting | bytes 17825792 | tf_op jit(solution)/shard_map/conv_general_dilated | solution.py:60
  435.2 1.5 select_reduce_fusion
  436.8 4.1 slice.16
  440.9 0.1 reduce_sum.37
  441.0 11.5 %copy.31 = f32[8,8,1,128,256]{4,0,3,1,2:T(8,128)} copy(f32[8,8,1,128,256]{4,1,3,0,2:T(8,128)} %slice.16) | data formatting | bytes 16777216 | tf_op jit(solution)/shard_map/conv_general_dilated | solution.py:60
  452.5 62.4 %psum.15 = f32[32]{0:T(128)S(1)} all-reduce(f32[32]{0:T(128)S(1)} %reduce_sum.37), channel_id=1, replica_groups=mesh['tm'=32,'rows'=4] {'tm','rows'}, use_global_device_ids=true, to_apply=%region_5.6 | all-reduce | flops 32 | bytes 256 | tf_op jit(solution)/shard_map/psum | solution.py:85
  515.2 6.9 %fusion.5 = bf16[4,64,8,2,2,256]{5,1,4,3,0,2:T(8,128)(2,1)S(1)} fusion(f32[256]{0:T(256)S(1)} %copy-done.4, f32[256]{0:T(256)S(1)} %copy-done.5, f32[256]{0:T(256)S(1)} %div.28, f32[256]{0:T(256)S(1)} %sub.32, f32[8,4,2,64,2,256]{5,0,4,3,2,1:T(8,128)} %bitcast.27), kind=kLoop, calls=%fused_computation.17 | loop fusion | flops 18874368 | bytes 12587008 | tf_op jit(solution)/shard_map/transpose | solution.py:93
  522.0 6.4 %copy.37 = bf16[4,64,8,2,2,256]{5,4,3,2,0,1:T(2,128)(2,1)} copy(bf16[4,64,8,2,2,256]{5,1,4,3,0,2:T(8,128)(2,1)S(1)} %fusion.5) | data formatting | bytes 8388608 | tf_op jit(solution)/shard_map/reshape | solution.py:94
  528.4 7.7 %reshape.33 = bf16[4,64,8,1024]{3,2,0,1:T(8,128)(2,1)} reshape(bf16[4,64,8,2,2,256]{5,4,3,2,0,1:T(2,128)(2,1)} %copy.37) | data formatting | bytes 8388608 | tf_op jit(solution)/shard_map/reshape | solution.py:94
  536.1 58.5 %all_to_all.18 = bf16[4,64,8,1024]{3,2,0,1:T(8,128)(2,1)S(1)} all-to-all(bf16[4,64,8,1024]{3,2,0,1:T(8,128)(2,1)} %reshape.33), channel_id=1, replica_groups=mesh['tm'=32,'rows'=4] {'tm'}, dimensions={1} | all-to-all | bytes 8388608 | tf_op jit(solution)/shard_map/all_to_all | solution.py:95
  594.6 2.5 copy.52
  (25 shorter events, 0.8 us)
Async XLA Ops:
  0.0 333.5 %copy-start = (bf16[3,3,3,128,256]{4,3,2,1,0:T(8,128)(2,1)S(1)}, bf16[3,3,3,128,256]{4,3,2,1,0:T(8,128)(2,1)}, u32[]{:S(2)}) copy-start(bf16[3,3,3,128,256]{4,3,2,1,0:T(8,128)(2,1)} %param.5) | copy-start | bytes 5308420
  4.3 94.2 %collective-permute-start = (f32[8,8,128,128]{3,2,1,0:T(8,128)}, f32[8,8,128,128]{3,2,1,0:T(8,128)}, u32[]{:S(2)}, u32[]{:S(2)}) collective-permute-start(f32[8,8,128,128]{3,2,1,0:T(8,128)} %convert_element_type.12), channel_id=1, source_target_pairs={{0,4},{4,0},{8,12},{12,8},{16,20},{20,16},{24,28},{28,24},{32,36},... | collective-permute-start | bytes 12582920 | tf_op jit(solution)/shard_map/ppermute | solution.py:17
  104.3 91.8 %collective-permute-start.1 = (f32[8,8,128,128]{3,2,1,0:T(8,128)}, f32[8,8,128,128]{3,2,1,0:T(8,128)}, u32[]{:S(2)}, u32[]{:S(2)}) collective-permute-start(f32[8,8,128,128]{3,2,1,0:T(8,128)} %multiply_select_fusion.1), channel_id=1, source_target_pairs={{0,8},{8,0},{4,12},{12,4},{16,24},{24,16},{20,28},{28,20},{32,40},... | collective-permute-start | bytes 12582920 | tf_op jit(solution)/shard_map/ppermute | solution.py:17
  203.0 92.4 %collective-permute-start.2 = (f32[8,8,128,128]{3,2,1,0:T(8,128)}, f32[8,8,128,128]{3,2,1,0:T(8,128)}, u32[]{:S(2)}, u32[]{:S(2)}) collective-permute-start(f32[8,8,128,128]{3,2,1,0:T(8,128)} %multiply_select_fusion), channel_id=1, source_target_pairs={{0,16},{16,0},{4,20},{20,4},{8,24},{24,8},{12,28},{28,12},{32,48},... | collective-permute-start | bytes 12582920 | tf_op jit(solution)/shard_map/ppermute | solution.py:17
  299.9 13.5 %collective-permute-start.3 = (bf16[2,8,128,128]{3,2,1,0:T(8,128)(2,1)S(1)}, bf16[2,8,128,128]{3,2,1,0:T(8,128)(2,1)S(1)}, u32[]{:S(2)}, u32[]{:S(2)}) collective-permute-start(bf16[2,8,128,128]{3,2,1,0:T(8,128)(2,1)S(1)} %slice.14), channel_id=1, source_target_pairs={{0,4},{4,8},{8,12},{12,16},{16,20},{20,24},{24,28},{28,32},{32,36}... | collective-permute-start | bytes 1572872 | tf_op jit(solution)/shard_map/ppermute | solution.py:23
  313.5 2.6 collective-permute-start.4
  314.9 4.4 collective-permute-start.5
  330.4 3.2 copy-start.3
  428.8 6.4 %copy-start.2 = (f32[8,8,8,17,256]{4,2,3,1,0:T(8,128)S(1)}, f32[8,8,8,17,256]{4,2,3,1,0:T(8,128)}, u32[]{:S(2)}) copy-start(f32[8,8,8,17,256]{4,2,3,1,0:T(8,128)} %get-tuple-element.8) | copy-start | bytes 26738692
  441.0 74.1 %copy-start.4 = (f32[256]{0:T(256)S(1)}, f32[256]{0:T(256)}, u32[]{:S(2)}) copy-start(f32[256]{0:T(256)} %param.7) | copy-start | bytes 3076
  441.0 74.1 %copy-start.5 = (f32[256]{0:T(256)S(1)}, f32[256]{0:T(256)}, u32[]{:S(2)}) copy-start(f32[256]{0:T(256)} %param.6) | copy-start | bytes 3076
  594.6 2.5 copy-start.1
where the time goes:
time: 598 us; the launch traced here: 597 us
  waiting for transfers between devices  282 us (47%)
  blocking collectives  197 us (33%)
  local copies, waits for them, and re-layouts  51 us (9%)
  other arithmetic  32.4 us (5%)
  matrix products  19 us (3%)
  starting transfers between devices  15.6 us (3%)
    ppermute x3, waiting for transfers between devices, from_partner(): return lax.ppermute(block, axis, route)  270 us
    psum x1, blocking collectives, per_device(): group_total = lax.psum(local_sums, ('tm', 'rows'))  75.9 us
    psum x1, blocking collectives, per_device(): lax.psum(jnp.sum(centered * centered, axis=(0, 1, 2, 4)), ('tm', 'rows'))  62.4 us
    all_to_all x1, blocking collectives, per_device(): lax.all_to_all(arranged, 'tm', split_axis=1, concat_axis=2, tiled=True)  58.5 us
    conv_general_dilated x6, local copies, waits for them, and re-layouts, per_device(): lax.conv_general_dilated(padded[None], conv_weight, (1, 1, 1), 'VALID', d...  31.9 us
    conv_general_dilated x1, matrix products, per_device(): lax.conv_general_dilated(padded[None], conv_weight, (1, 1, 1), 'VALID', d...  19 us
    reshape x2, local copies, waits for them, and re-layouts, per_device(): arranged.reshape(out_height // 2, out_width // 2, out_frames, 4 * out_cha...  14.1 us
    select_n x2, other arithmetic, per_device(): jnp.where(is_upper, (partner - current) * inv_root, (current + partner) *...  12.8 us
  transfers between devices with their start and end apart: 6, of which 5 were waited for; matrix products, arithmetic and copies ran while one was open for 0% of the time, Pallas kernels for 0%

commit v1 on v0

--- a/solution.py
+++ b/solution.py
@@ -79,7 +79,13 @@
         * lax.axis_size("rows")
     )
     local_sums = jnp.sum(groups, axis=(0, 1, 2, 4))
-    group_total = lax.psum(local_sums, ("tm", "rows"))
+
+    def frame_produce(local_x, along_axis, lane_axis="tm"):
+        for c in (along_axis, lane_axis):
+            local_x = lax.psum(local_x, c)
+        return local_x
+
+    group_total = frame_produce(local_sums, "rows")
     group_mean = group_total / entries
     centered = groups - group_mean[:, None]
     squares = lax.psum(jnp.sum(centered * centered, axis=(0, 1, 2, 4)), ("tm", "rows"))

time: 598 us -> 632 us (1.057)
  blocking collectives: 197 us -> 231 us
    psum x1 -> x2, blocking collectives: 75.9 us -> 110 us  [frame_produce(): local_x = lax.psum(local_x, c)]
where the time goes in v1:
time: 632 us; the launch traced here: 631 us
  waiting for transfers between devices  282 us (45%)
  blocking collectives  231 us (37%)
  local copies, waits for them, and re-layouts  51.1 us (8%)
  other arithmetic  32.4 us (5%)
  matrix products  19 us (3%)
  starting transfers between devices  15.6 us (2%)
    ppermute x3, waiting for transfers between devices, from_partner(): return lax.ppermute(block, axis, route)  270 us
    psum x2, blocking collectives, frame_produce(): local_x = lax.psum(local_x, c)  110 us
    psum x1, blocking collectives, per_device(): lax.psum(jnp.sum(centered * centered, axis=(0, 1, 2, 4)), ('tm', 'rows'))  62.7 us
    all_to_all x1, blocking collectives, per_device(): lax.all_to_all(arranged, 'tm', split_axis=1, concat_axis=2, tiled=True)  58 us
    conv_general_dilated x6, local copies, waits for them, and re-layouts, per_device(): lax.conv_general_dilated(padded[None], conv_weight, (1, 1, 1), 'VALID', d...  31.9 us
    conv_general_dilated x1, matrix products, per_device(): lax.conv_general_dilated(padded[None], conv_weight, (1, 1, 1), 'VALID', d...  19 us
    reshape x2, local copies, waits for them, and re-layouts, per_device(): arranged.reshape(out_height // 2, out_width // 2, out_frames, 4 * out_cha...  14.1 us
    select_n x2, other arithmetic, per_device(): jnp.where(is_upper, (partner - current) * inv_root, (current + partner) *...  12.8 us
  transfers between devices with their start and end apart: 6, of which 5 were waited for; matrix products, arithmetic and copies ran while one was open for 0% of the time, Pallas kernels for 0%

profile of v1, /device:TPU:0, one launch (start us, length us, event | category | flops | bytes accessed | tf_op | source)
XLA Modules:
  0.0 631.1 jit_solution(9237313571272716863)
XLA Ops:
  0.0 4.3 convert_element_type.12
  4.3 3.3 collective-permute-start
  7.5 90.9 %collective-permute-done = f32[8,8,128,128]{3,2,1,0:T(8,128)} collective-permute-done((f32[8,8,128,128]{3,2,1,0:T(8,128)}, f32[8,8,128,128]{3,2,1,0:T(8,128)}, u32[]{:S(2)}, u32[]{:S(2)}) %collective-permute-start) | collective-permute-done | bytes 4194336 | tf_op jit(solution)/shard_map/ppermute | solution.py:17
  98.4 5.9 multiply_select_fusion.1
  104.3 1.5 collective-permute-start.1
  105.9 90.2 %collective-permute-done.1 = f32[8,8,128,128]{3,2,1,0:T(8,128)} collective-permute-done((f32[8,8,128,128]{3,2,1,0:T(8,128)}, f32[8,8,128,128]{3,2,1,0:T(8,128)}, u32[]{:S(2)}, u32[]{:S(2)}) %collective-permute-start.1) | collective-permute-done | bytes 4194336 | tf_op jit(solution)/shard_map/ppermute | solution.py:17
  196.1 6.9 %multiply_select_fusion = f32[8,8,128,128]{3,2,1,0:T(8,128)} fusion(f32[8,8,128,128]{3,2,1,0:T(8,128)} %multiply_select_fusion.1, f32[8,8,128,128]{3,2,1,0:T(8,128)} %collective-permute-done.1, pred[]{:T(512)S(6)} %eq.10), kind=kLoop, calls=%fused_computation.15 | loop fusion | flops 5242880 | bytes 12582913 | tf_op jit(solution)/shard_map/jit(_where)/select_n | solution.py:51
  203.0 3.0 collective-permute-start.2
  206.1 89.3 %collective-permute-done.2 = f32[8,8,128,128]{3,2,1,0:T(8,128)} collective-permute-done((f32[8,8,128,128]{3,2,1,0:T(8,128)}, f32[8,8,128,128]{3,2,1,0:T(8,128)}, u32[]{:S(2)}, u32[]{:S(2)}) %collective-permute-start.2) | collective-permute-done | bytes 4194336 | tf_op jit(solution)/shard_map/ppermute | solution.py:17
  295.4 4.5 select_convert_fusion
  299.9 5.1 collective-permute-start.3
  305.1 8.4 %collective-permute-done.3 = bf16[2,8,128,128]{3,2,1,0:T(8,128)(2,1)S(1)} collective-permute-done((bf16[2,8,128,128]{3,2,1,0:T(8,128)(2,1)S(1)}, bf16[2,8,128,128]{3,2,1,0:T(8,128)(2,1)S(1)}, u32[]{:S(2)}, u32[]{:S(2)}) %collective-permute-start.3) | collective-permute-done | bytes 524320 | tf_op jit(solution)/shard_map/ppermute | solution.py:23
  313.5 1.3 collective-permute-start.4
  314.9 1.3 collective-permute-start.5
  316.2 3.1 collective-permute-done.5
  319.3 2.1 fusion.13
  321.4 2.0 pad.5
  323.4 6.9 %reshape.19 = bf16[10,10,1,8,17,128]{5,4,3,1,0,2:T(8,128)(2,1)} reshape(bf16[10,10,1,136,128]{4,3,1,0,2:T(8,128)(2,1)} %pad.5) | data formatting | bytes 6963200 | tf_op jit(solution)/shard_map/conv_general_dilated | solution.py:60
  330.4 3.0 copy.29
  333.5 19.0 %select_reduce_fusion.1 = (f32[256]{0:T(256)S(1)}, f32[8,8,8,17,256]{4,2,3,1,0:T(8,128)}) fusion(pred[8,17]{0,1:T(8,128)(4,1)S(1)} %copy-done.3, bf16[3,3,3,128,256]{4,3,2,1,0:T(8,128)(2,1)S(1)} %copy-done, bf16[10,10,1,7,2,128]{5,3,4,1,0,2:T(8,128)(2,1)S(1)} %slice.15, bf16[10,10,1,8,17,128]{5,3,4,1,0,2:T(8,128)(2,1)S(1)} %copy.29), kind=kOutput, calls=%fused_computation.3 | convolution fusion | flops 15419842560 | bytes 14523528 | tf_op jit(solution)/shard_map/conv_general_dilated | solution.py:60
  352.8 11.0 %psum.21 = f32[32]{0:T(128)S(1)} all-reduce(f32[32]{0:T(128)S(1)} %reduce_sum.25), channel_id=1, replica_groups=mesh['tm'=32,'rows'=4] {'rows'}, use_global_device_ids=true, to_apply=%region_2.3 | all-reduce | flops 32 | bytes 256 | tf_op jit(solution)/shard_map/psum | solution.py:85
  363.8 99.3 %psum.22 = f32[32]{0:T(128)S(1)} all-reduce(f32[32]{0:T(128)S(1)} %psum.21), channel_id=1, replica_groups=mesh['tm'=32,'rows'=4] {'tm'}, use_global_device_ids=true, to_apply=%region_3.4 | all-reduce | flops 32 | bytes 256 | tf_op jit(solution)/shard_map/psum | solution.py:85
  463.3 6.3 %copy.30 = f32[8,8,8,17,256]{4,1,3,2,0:T(8,128)S(1)} copy(f32[8,8,8,17,256]{4,2,3,1,0:T(8,128)} %get-tuple-element.8) | data formatting | bytes 17825792 | tf_op jit(solution)/shard_map/conv_general_dilated | solution.py:60
  469.6 1.5 select_reduce_fusion
  471.2 4.1 slice.16
  475.4 11.5 %copy.31 = f32[8,8,1,128,256]{4,0,3,1,2:T(8,128)} copy(f32[8,8,1,128,256]{4,1,3,0,2:T(8,128)} %slice.16) | data formatting | bytes 16777216 | tf_op jit(solution)/shard_map/conv_general_dilated | solution.py:60
  486.9 62.7 %psum.23 = f32[32]{0:T(128)S(1)} all-reduce(f32[32]{0:T(128)S(1)} %reduce_sum.37), channel_id=1, replica_groups=mesh['tm'=32,'rows'=4] {'tm','rows'}, use_global_device_ids=true, to_apply=%region_6.7 | all-reduce | flops 32 | bytes 256 | tf_op jit(solution)/shard_map/psum | solution.py:91
  549.8 6.9 %fusion.5 = bf16[4,64,8,2,2,256]{5,1,4,3,0,2:T(8,128)(2,1)S(1)} fusion(f32[256]{0:T(256)S(1)} %copy-done.4, f32[256]{0:T(256)S(1)} %copy-done.5, f32[256]{0:T(256)S(1)} %div.28, f32[256]{0:T(256)S(1)} %sub.32, f32[8,4,2,64,2,256]{5,0,4,3,2,1:T(8,128)} %bitcast.27), kind=kLoop, calls=%fused_computation.17 | loop fusion | flops 18874368 | bytes 12587008 | tf_op jit(solution)/shard_map/transpose | solution.py:99
  556.6 6.4 %copy.37 = bf16[4,64,8,2,2,256]{5,4,3,2,0,1:T(2,128)(2,1)} copy(bf16[4,64,8,2,2,256]{5,1,4,3,0,2:T(8,128)(2,1)S(1)} %fusion.5) | data formatting | bytes 8388608 | tf_op jit(solution)/shard_map/reshape | solution.py:100
  563.0 7.7 %reshape.33 = bf16[4,64,8,1024]{3,2,0,1:T(8,128)(2,1)} reshape(bf16[4,64,8,2,2,256]{5,4,3,2,0,1:T(2,128)(2,1)} %copy.37) | data formatting | bytes 8388608 | tf_op jit(solution)/shard_map/reshape | solution.py:100
  570.7 58.0 %all_to_all.18 = bf16[4,64,8,1024]{3,2,0,1:T(8,128)(2,1)S(1)} all-to-all(bf16[4,64,8,1024]{3,2,0,1:T(8,128)(2,1)} %reshape.33), channel_id=1, replica_groups=mesh['tm'=32,'rows'=4] {'tm'}, dimensions={1} | all-to-all | bytes 8388608 | tf_op jit(solution)/shard_map/all_to_all | solution.py:101
  628.7 2.5 copy.52
  (26 shorter events, 1.0 us)
Async XLA Ops:
  0.0 333.5 %copy-start = (bf16[3,3,3,128,256]{4,3,2,1,0:T(8,128)(2,1)S(1)}, bf16[3,3,3,128,256]{4,3,2,1,0:T(8,128)(2,1)}, u32[]{:S(2)}) copy-start(bf16[3,3,3,128,256]{4,3,2,1,0:T(8,128)(2,1)} %param.5) | copy-start | bytes 5308420
  4.3 94.2 %collective-permute-start = (f32[8,8,128,128]{3,2,1,0:T(8,128)}, f32[8,8,128,128]{3,2,1,0:T(8,128)}, u32[]{:S(2)}, u32[]{:S(2)}) collective-permute-start(f32[8,8,128,128]{3,2,1,0:T(8,128)} %convert_element_type.12), channel_id=1, source_target_pairs={{0,4},{4,0},{8,12},{12,8},{16,20},{20,16},{24,28},{28,24},{32,36},... | collective-permute-start | bytes 12582920 | tf_op jit(solution)/shard_map/ppermute | solution.py:17
  104.3 91.8 %collective-permute-start.1 = (f32[8,8,128,128]{3,2,1,0:T(8,128)}, f32[8,8,128,128]{3,2,1,0:T(8,128)}, u32[]{:S(2)}, u32[]{:S(2)}) collective-permute-start(f32[8,8,128,128]{3,2,1,0:T(8,128)} %multiply_select_fusion.1), channel_id=1, source_target_pairs={{0,8},{8,0},{4,12},{12,4},{16,24},{24,16},{20,28},{28,20},{32,40},... | collective-permute-start | bytes 12582920 | tf_op jit(solution)/shard_map/ppermute | solution.py:17
  203.0 92.4 %collective-permute-start.2 = (f32[8,8,128,128]{3,2,1,0:T(8,128)}, f32[8,8,128,128]{3,2,1,0:T(8,128)}, u32[]{:S(2)}, u32[]{:S(2)}) collective-permute-start(f32[8,8,128,128]{3,2,1,0:T(8,128)} %multiply_select_fusion), channel_id=1, source_target_pairs={{0,16},{16,0},{4,20},{20,4},{8,24},{24,8},{12,28},{28,12},{32,48},... | collective-permute-start | bytes 12582920 | tf_op jit(solution)/shard_map/ppermute | solution.py:17
  299.9 13.5 %collective-permute-start.3 = (bf16[2,8,128,128]{3,2,1,0:T(8,128)(2,1)S(1)}, bf16[2,8,128,128]{3,2,1,0:T(8,128)(2,1)S(1)}, u32[]{:S(2)}, u32[]{:S(2)}) collective-permute-start(bf16[2,8,128,128]{3,2,1,0:T(8,128)(2,1)S(1)} %slice.14), channel_id=1, source_target_pairs={{0,4},{4,8},{8,12},{12,16},{16,20},{20,24},{24,28},{28,32},{32,36}... | collective-permute-start | bytes 1572872 | tf_op jit(solution)/shard_map/ppermute | solution.py:23
  313.5 2.6 collective-permute-start.4
  314.9 4.4 collective-permute-start.5
  330.4 3.2 copy-start.3
  463.3 6.4 %copy-start.2 = (f32[8,8,8,17,256]{4,2,3,1,0:T(8,128)S(1)}, f32[8,8,8,17,256]{4,2,3,1,0:T(8,128)}, u32[]{:S(2)}) copy-start(f32[8,8,8,17,256]{4,2,3,1,0:T(8,128)} %get-tuple-element.8) | copy-start | bytes 26738692
  475.4 74.3 %copy-start.4 = (f32[256]{0:T(256)S(1)}, f32[256]{0:T(256)}, u32[]{:S(2)}) copy-start(f32[256]{0:T(256)} %param.7) | copy-start | bytes 3076
  475.4 74.3 %copy-start.5 = (f32[256]{0:T(256)S(1)}, f32[256]{0:T(256)}, u32[]{:S(2)}) copy-start(f32[256]{0:T(256)} %param.6) | copy-start | bytes 3076
  628.7 2.5 copy-start.1
